TPU v7x, 32 devices: a whole 2x2x4 slice. The times are simulated.
32 devices in a mesh: groups: 2 (over x), dates: 16 (over z, y, core).
Axes of the slice: x: 2, y: 2, z: 4, core: 2. Of those that a mesh axis runs over, the one named last changes fastest.
Arguments:
- scenes: bfloat16 [64, 4, 64, 128], P(('groups', 'dates')), parts along dimension 0, may hold values from -10 to 14
- cloud_mask: int32 [64, 64, 128], P(('groups', 'dates')), parts along dimension 0, may hold values 0 or 1
- region: int32 [128, 128], P('groups'), parts along dimension 0, may hold values from 0 to 7
Outputs:
- smoothed: bfloat16 [64, 4, 64, 128], P('groups', None, 'dates'), parts along dimension 0
- similarity: float32 [64, 32], P(('groups', 'dates')), parts along dimension 0
There are 2 independent parts, one for each index of `groups`. A program takes and returns all parts, laid end to end along the dimension named above; each array names one. Nothing has to cross between parts.
All inputs are finite; a program needn't handle non-finite values. No bound on the sum of `cloud_mask` on one device may be relied on, other than what follows from the above.
Results may differ from a plain program's by a relative error of at most 0.0065.
Values may be sent and summed in bfloat16 or wider, within the bound.
A program may use at most 64 MiB of HBM per device.

v0:
```python
import jax
import jax.numpy as jnp
from jax import lax
from jax.sharding import PartitionSpec as P

REGIONS = 8
STEPS = 4


lam_space = 0.2
lam_time = 0.08


def extended(block, sides, width):
    for axis, dim in sides:
        count = lax.axis_size(axis)
        forward = [(i, i + 1) for i in range(count - 1)]
        backward = [(target, source) for source, target in forward]
        low = lax.ppermute(
            lax.slice_in_dim(block, block.shape[dim] - width, None, axis=dim), axis, forward
        )
        high = lax.ppermute(lax.slice_in_dim(block, 0, width, axis=dim), axis, backward)
        block = jnp.concatenate([low, block, high], axis=dim)
    return block


def edge_flux(difference):
    return difference / (1.0 + difference * difference)


def advance(current, padded_rows, padded_dates, row_weight, col_weight, date_weight):
    row_flux = lam_space * row_weight * edge_flux(padded_rows[:, :, 1:] - padded_rows[:, :, :-1])
    padded_cols = jnp.pad(current, ((0, 0), (0, 0), (0, 0), (1, 1)))
    col_flux = lam_space * col_weight * edge_flux(padded_cols[..., 1:] - padded_cols[..., :-1])
    date_flux = (
        lam_time
        * date_weight[:, None, None, None]
        * edge_flux(padded_dates[1:] - padded_dates[:-1])
    )
    return (
        current
        + (row_flux[:, :, 1:] - row_flux[:, :, :-1])
        + (col_flux[..., 1:] - col_flux[..., :-1])
        + (date_flux[1:] - date_flux[:-1])
    )


def local(scenes, cloud_mask, region):
    date_dev = scenes.shape[0]
    devices = lax.axis_size("dates")
    dates_all = date_dev * devices
    clear_half = cloud_mask.astype(jnp.bfloat16)
    masked = scenes * clear_half[:, None]
    labels = lax.broadcasted_iota(jnp.int32, (REGIONS, 1, 1), 0)
    member = region[None] == labels
    onehot_half = member.astype(jnp.bfloat16)
    onehot_full = member.astype(jnp.float32)
    sums = jnp.einsum("dbrc,grc->dbg", masked, onehot_half, preferred_element_type=jnp.float32)
    counts = jnp.einsum("drc,grc->dg", clear_half, onehot_half, preferred_element_type=jnp.float32)
    means = sums / (counts[:, None, :] + 1.0)
    pixel_mean = jnp.einsum("dbg,grc->dbrc", means, onehot_full, precision=lax.Precision.HIGHEST)
    anomaly = (
        cloud_mask.astype(jnp.float32)[:, None] * (scenes.astype(jnp.float32) - pixel_mean)
    ).astype(jnp.bfloat16)
    land_padded = jnp.pad((region > 0).astype(jnp.float32), 1)
    row_weight = land_padded[1:, 1:-1] * land_padded[:-1, 1:-1]
    col_weight = land_padded[1:-1, 1:] * land_padded[1:-1, :-1]
    lower = jnp.arange(date_dev + 1, dtype=jnp.int32) + lax.axis_index("dates") * date_dev - 1
    date_weight = ((lower >= 0) & (lower + 1 <= dates_all - 1)).astype(jnp.float32)
    current = anomaly.astype(jnp.float32)
    for step_index in range(STEPS):
        padded_dates = extended(current.astype(jnp.bfloat16), (("dates", 0),), 1).astype(
            current.dtype
        )
        padded_rows = jnp.pad(current, ((0, 0), (0, 0), (1, 1), (0, 0)))
        current = advance(current, padded_rows, padded_dates, row_weight, col_weight, date_weight)
    smoothed = lax.all_to_all(
        current.astype(jnp.bfloat16), "dates", split_axis=2, concat_axis=0, tiled=True
    )
    flat = smoothed.reshape(smoothed.shape[0], -1)
    total_features = flat.shape[1] * devices
    product = lax.dot_general(
        flat, flat, (((1,), (1,)), ((), ())), preferred_element_type=jnp.float32
    )
    similarity = lax.psum_scatter(
        product / total_features, "dates", scatter_dimension=0, tiled=True
    )
    return (smoothed, similarity)


def solution(mesh):
    in_specs = (
        P(("groups", "dates"), None, None, None),
        P(("groups", "dates"), None, None),
        P("groups", None),
    )
    out_specs = (P("groups", None, "dates", None), P(("groups", "dates"), None))
    return jax.shard_map(local, mesh=mesh, in_specs=in_specs, out_specs=out_specs, check_vma=False)
```

profile of v0, /device:TPU:0, one launch (start us, length us, event | category | flops | bytes accessed | tf_op | source)
XLA Modules:
  0.0 115.5 jit_solution(15377025040289881221)
XLA Ops:
  0.6 0.9 fusion.55
  1.6 0.7 copy-done.2
  2.5 0.4 fusion.3
  2.9 0.4 fusion.56
  3.3 2.4 %collective-permute-start = (bf16[1,4,64,128]{3,1,2,0:T(4,128)(2,1)S(1)}, bf16[1,4,64,128]{3,1,2,0:T(4,128)(2,1)S(1)}, u32[]{:S(2)}, u32[]{:S(2)}) collective-permute-start(bf16[1,4,64,128]{3,1,2,0:T(4,128)(2,1)S(1)} %get-tuple-element.16), channel_id=1, source_target_pairs={{0,1},{1,2},{2,3},{3,4},{4,5},{5,6},{6,7},{7,8},{8,9},{9,10},{10,1... | collective-permute-start | bytes 196616 | tf_op jit(solution)/shard_map/ppermute | solution.py:19
  5.7 1.3 %collective-permute-start.1 = (bf16[1,4,64,128]{3,1,2,0:T(4,128)(2,1)S(1)}, bf16[1,4,64,128]{3,1,2,0:T(4,128)(2,1)S(1)}, u32[]{:S(2)}, u32[]{:S(2)}) collective-permute-start(bf16[1,4,64,128]{3,1,2,0:T(4,128)(2,1)S(1)} %get-tuple-element.17), channel_id=1, source_target_pairs={{1,0},{2,1},{3,2},{4,3},{5,4},{6,5},{7,6},{8,7},{9,8},{10,9},{11,1... | collective-permute-start | bytes 196616 | tf_op jit(solution)/shard_map/ppermute | solution.py:22
  7.8 3.2 %collective-permute-done.1 = bf16[1,4,64,128]{3,1,2,0:T(4,128)(2,1)S(1)} collective-permute-done((bf16[1,4,64,128]{3,1,2,0:T(4,128)(2,1)S(1)}, bf16[1,4,64,128]{3,1,2,0:T(4,128)(2,1)S(1)}, u32[]{:S(2)}, u32[]{:S(2)}) %collective-permute-start.1) | collective-permute-done | bytes 65568 | tf_op jit(solution)/shard_map/ppermute | solution.py:22
  11.7 4.8 %collective-permute-start.2 = (bf16[1,4,64,128]{3,1,2,0:T(4,128)(2,1)S(1)}, bf16[1,4,64,128]{3,1,2,0:T(4,128)(2,1)S(1)}, u32[]{:S(2)}, u32[]{:S(2)}) collective-permute-start(bf16[1,4,64,128]{3,1,2,0:T(4,128)(2,1)S(1)} %get-tuple-element.14), channel_id=1, source_target_pairs={{0,1},{1,2},{2,3},{3,4},{4,5},{5,6},{6,7},{7,8},{8,9},{9,10},{10,1... | collective-permute-start | bytes 196616 | tf_op jit(solution)/shard_map/ppermute | solution.py:19
  16.5 1.3 %collective-permute-start.3 = (bf16[1,4,64,128]{3,1,2,0:T(4,128)(2,1)S(1)}, bf16[1,4,64,128]{3,1,2,0:T(4,128)(2,1)S(1)}, u32[]{:S(2)}, u32[]{:S(2)}) collective-permute-start(bf16[1,4,64,128]{3,1,2,0:T(4,128)(2,1)S(1)} %get-tuple-element.15), channel_id=1, source_target_pairs={{1,0},{2,1},{3,2},{4,3},{5,4},{6,5},{7,6},{8,7},{9,8},{10,9},{11,1... | collective-permute-start | bytes 196616 | tf_op jit(solution)/shard_map/ppermute | solution.py:22
  18.3 1.4 %collective-permute-done.3 = bf16[1,4,64,128]{3,1,2,0:T(4,128)(2,1)S(1)} collective-permute-done((bf16[1,4,64,128]{3,1,2,0:T(4,128)(2,1)S(1)}, bf16[1,4,64,128]{3,1,2,0:T(4,128)(2,1)S(1)}, u32[]{:S(2)}, u32[]{:S(2)}) %collective-permute-start.3) | collective-permute-done | bytes 65568 | tf_op jit(solution)/shard_map/ppermute | solution.py:22
  20.4 5.1 %collective-permute-start.4 = (bf16[1,4,64,128]{3,1,2,0:T(4,128)(2,1)S(1)}, bf16[1,4,64,128]{3,1,2,0:T(4,128)(2,1)S(1)}, u32[]{:S(2)}, u32[]{:S(2)}) collective-permute-start(bf16[1,4,64,128]{3,1,2,0:T(4,128)(2,1)S(1)} %get-tuple-element.12), channel_id=1, source_target_pairs={{0,1},{1,2},{2,3},{3,4},{4,5},{5,6},{6,7},{7,8},{8,9},{9,10},{10,1... | collective-permute-start | bytes 196616 | tf_op jit(solution)/shard_map/ppermute | solution.py:19
  25.5 1.3 %collective-permute-start.5 = (bf16[1,4,64,128]{3,1,2,0:T(4,128)(2,1)S(1)}, bf16[1,4,64,128]{3,1,2,0:T(4,128)(2,1)S(1)}, u32[]{:S(2)}, u32[]{:S(2)}) collective-permute-start(bf16[1,4,64,128]{3,1,2,0:T(4,128)(2,1)S(1)} %get-tuple-element.13), channel_id=1, source_target_pairs={{1,0},{2,1},{3,2},{4,3},{5,4},{6,5},{7,6},{8,7},{9,8},{10,9},{11,1... | collective-permute-start | bytes 196616 | tf_op jit(solution)/shard_map/ppermute | solution.py:22
  27.3 1.4 %collective-permute-done.5 = bf16[1,4,64,128]{3,1,2,0:T(4,128)(2,1)S(1)} collective-permute-done((bf16[1,4,64,128]{3,1,2,0:T(4,128)(2,1)S(1)}, bf16[1,4,64,128]{3,1,2,0:T(4,128)(2,1)S(1)}, u32[]{:S(2)}, u32[]{:S(2)}) %collective-permute-start.5) | collective-permute-done | bytes 65568 | tf_op jit(solution)/shard_map/ppermute | solution.py:22
  29.3 5.3 %collective-permute-start.6 = (bf16[1,4,64,128]{3,1,2,0:T(4,128)(2,1)S(1)}, bf16[1,4,64,128]{3,1,2,0:T(4,128)(2,1)S(1)}, u32[]{:S(2)}, u32[]{:S(2)}) collective-permute-start(bf16[1,4,64,128]{3,1,2,0:T(4,128)(2,1)S(1)} %get-tuple-element.10), channel_id=1, source_target_pairs={{0,1},{1,2},{2,3},{3,4},{4,5},{5,6},{6,7},{7,8},{8,9},{9,10},{10,1... | collective-permute-start | bytes 196616 | tf_op jit(solution)/shard_map/ppermute | solution.py:19
  34.6 1.3 %collective-permute-start.7 = (bf16[1,4,64,128]{3,1,2,0:T(4,128)(2,1)S(1)}, bf16[1,4,64,128]{3,1,2,0:T(4,128)(2,1)S(1)}, u32[]{:S(2)}, u32[]{:S(2)}) collective-permute-start(bf16[1,4,64,128]{3,1,2,0:T(4,128)(2,1)S(1)} %get-tuple-element.11), channel_id=1, source_target_pairs={{1,0},{2,1},{3,2},{4,3},{5,4},{6,5},{7,6},{8,7},{9,8},{10,9},{11,1... | collective-permute-start | bytes 196616 | tf_op jit(solution)/shard_map/ppermute | solution.py:22
  36.4 1.4 %collective-permute-done.7 = bf16[1,4,64,128]{3,1,2,0:T(4,128)(2,1)S(1)} collective-permute-done((bf16[1,4,64,128]{3,1,2,0:T(4,128)(2,1)S(1)}, bf16[1,4,64,128]{3,1,2,0:T(4,128)(2,1)S(1)}, u32[]{:S(2)}, u32[]{:S(2)}) %collective-permute-start.7) | collective-permute-done | bytes 65568 | tf_op jit(solution)/shard_map/ppermute | solution.py:22
  38.4 0.7 copy.12
  39.1 8.9 %all-to-all-start = ((bf16[2,4,64,128]{3,1,0,2:T(4,128)(2,1)}), bf16[2,4,64,128]{3,1,0,2:T(4,128)(2,1)S(1)}, u32[]{:S(2)}, u32[]{:S(2)}) async-start(bf16[2,4,64,128]{3,1,0,2:T(4,128)(2,1)} %copy.12), calls=%async_computation | async-start | bytes 262144 | tf_op jit(solution)/shard_map/all_to_all | solution.py:77
  48.0 0.6 copy-done.3
  48.6 0.6 dynamic-slice
  49.9 6.0 %all-to-all-done = bf16[2,4,64,128]{3,1,0,2:T(4,128)(2,1)S(1)} async-done(((bf16[2,4,64,128]{3,1,0,2:T(4,128)(2,1)}), bf16[2,4,64,128]{3,1,0,2:T(4,128)(2,1)S(1)}, u32[]{:S(2)}, u32[]{:S(2)}) %all-to-all-start) | async-done | bytes 131104 | tf_op jit(solution)/shard_map/all_to_all | solution.py:77
  56.0 0.6 copy-done.1
  56.8 58.2 %all-reduce.9 = f32[32,32]{1,0:T(8,128)S(1)} all-reduce(f32[32,32]{1,0:T(8,128)S(1)} %convolution_multiply_fusion), channel_id=2, replica_groups=mesh['groups'=2,'dates'=16] {'dates'}, use_global_device_ids=true, to_apply=%region_0.1.clone | all-reduce | flops 1024 | bytes 8192
  114.9 0.6 constant_dynamic-slice_fusion
  (43 shorter events, 5.3 us)
Async XLA Ops:
  0.6 1.0 copy-start
  1.6 0.8 copy-start.2
  3.3 4.5 %collective-permute-start = (bf16[1,4,64,128]{3,1,2,0:T(4,128)(2,1)S(1)}, bf16[1,4,64,128]{3,1,2,0:T(4,128)(2,1)S(1)}, u32[]{:S(2)}, u32[]{:S(2)}) collective-permute-start(bf16[1,4,64,128]{3,1,2,0:T(4,128)(2,1)S(1)} %get-tuple-element.16), channel_id=1, source_target_pairs={{0,1},{1,2},{2,3},{3,4},{4,5},{5,6},{6,7},{7,8},{8,9},{9,10},{10,1... | collective-permute-start | bytes 196616 | tf_op jit(solution)/shard_map/ppermute | solution.py:19
  5.7 5.3 %collective-permute-start.1 = (bf16[1,4,64,128]{3,1,2,0:T(4,128)(2,1)S(1)}, bf16[1,4,64,128]{3,1,2,0:T(4,128)(2,1)S(1)}, u32[]{:S(2)}, u32[]{:S(2)}) collective-permute-start(bf16[1,4,64,128]{3,1,2,0:T(4,128)(2,1)S(1)} %get-tuple-element.17), channel_id=1, source_target_pairs={{1,0},{2,1},{3,2},{4,3},{5,4},{6,5},{7,6},{8,7},{9,8},{10,9},{11,1... | collective-permute-start | bytes 196616 | tf_op jit(solution)/shard_map/ppermute | solution.py:22
  11.7 6.6 %collective-permute-start.2 = (bf16[1,4,64,128]{3,1,2,0:T(4,128)(2,1)S(1)}, bf16[1,4,64,128]{3,1,2,0:T(4,128)(2,1)S(1)}, u32[]{:S(2)}, u32[]{:S(2)}) collective-permute-start(bf16[1,4,64,128]{3,1,2,0:T(4,128)(2,1)S(1)} %get-tuple-element.14), channel_id=1, source_target_pairs={{0,1},{1,2},{2,3},{3,4},{4,5},{5,6},{6,7},{7,8},{8,9},{9,10},{10,1... | collective-permute-start | bytes 196616 | tf_op jit(solution)/shard_map/ppermute | solution.py:19
  16.5 3.1 %collective-permute-start.3 = (bf16[1,4,64,128]{3,1,2,0:T(4,128)(2,1)S(1)}, bf16[1,4,64,128]{3,1,2,0:T(4,128)(2,1)S(1)}, u32[]{:S(2)}, u32[]{:S(2)}) collective-permute-start(bf16[1,4,64,128]{3,1,2,0:T(4,128)(2,1)S(1)} %get-tuple-element.15), channel_id=1, source_target_pairs={{1,0},{2,1},{3,2},{4,3},{5,4},{6,5},{7,6},{8,7},{9,8},{10,9},{11,1... | collective-permute-start | bytes 196616 | tf_op jit(solution)/shard_map/ppermute | solution.py:22
  20.4 6.9 %collective-permute-start.4 = (bf16[1,4,64,128]{3,1,2,0:T(4,128)(2,1)S(1)}, bf16[1,4,64,128]{3,1,2,0:T(4,128)(2,1)S(1)}, u32[]{:S(2)}, u32[]{:S(2)}) collective-permute-start(bf16[1,4,64,128]{3,1,2,0:T(4,128)(2,1)S(1)} %get-tuple-element.12), channel_id=1, source_target_pairs={{0,1},{1,2},{2,3},{3,4},{4,5},{5,6},{6,7},{7,8},{8,9},{9,10},{10,1... | collective-permute-start | bytes 196616 | tf_op jit(solution)/shard_map/ppermute | solution.py:19
  25.5 3.1 %collective-permute-start.5 = (bf16[1,4,64,128]{3,1,2,0:T(4,128)(2,1)S(1)}, bf16[1,4,64,128]{3,1,2,0:T(4,128)(2,1)S(1)}, u32[]{:S(2)}, u32[]{:S(2)}) collective-permute-start(bf16[1,4,64,128]{3,1,2,0:T(4,128)(2,1)S(1)} %get-tuple-element.13), channel_id=1, source_target_pairs={{1,0},{2,1},{3,2},{4,3},{5,4},{6,5},{7,6},{8,7},{9,8},{10,9},{11,1... | collective-permute-start | bytes 196616 | tf_op jit(solution)/shard_map/ppermute | solution.py:22
  29.3 7.0 %collective-permute-start.6 = (bf16[1,4,64,128]{3,1,2,0:T(4,128)(2,1)S(1)}, bf16[1,4,64,128]{3,1,2,0:T(4,128)(2,1)S(1)}, u32[]{:S(2)}, u32[]{:S(2)}) collective-permute-start(bf16[1,4,64,128]{3,1,2,0:T(4,128)(2,1)S(1)} %get-tuple-element.10), channel_id=1, source_target_pairs={{0,1},{1,2},{2,3},{3,4},{4,5},{5,6},{6,7},{7,8},{8,9},{9,10},{10,1... | collective-permute-start | bytes 196616 | tf_op jit(solution)/shard_map/ppermute | solution.py:19
  34.6 3.1 %collective-permute-start.7 = (bf16[1,4,64,128]{3,1,2,0:T(4,128)(2,1)S(1)}, bf16[1,4,64,128]{3,1,2,0:T(4,128)(2,1)S(1)}, u32[]{:S(2)}, u32[]{:S(2)}) collective-permute-start(bf16[1,4,64,128]{3,1,2,0:T(4,128)(2,1)S(1)} %get-tuple-element.11), channel_id=1, source_target_pairs={{1,0},{2,1},{3,2},{4,3},{5,4},{6,5},{7,6},{8,7},{9,8},{10,9},{11,1... | collective-permute-start | bytes 196616 | tf_op jit(solution)/shard_map/ppermute | solution.py:22
  39.1 16.8 %all-to-all-start = ((bf16[2,4,64,128]{3,1,0,2:T(4,128)(2,1)}), bf16[2,4,64,128]{3,1,0,2:T(4,128)(2,1)S(1)}, u32[]{:S(2)}, u32[]{:S(2)}) async-start(bf16[2,4,64,128]{3,1,0,2:T(4,128)(2,1)} %copy.12), calls=%async_computation | async-start | bytes 262144 | tf_op jit(solution)/shard_map/all_to_all | solution.py:77
  48.0 0.7 copy-start.3
  55.9 0.7 copy-start.1
where the time goes:
time: 116 us
  blocking collectives  58.2 us (50%)
  starting transfers between devices  31.7 us (27%)
  waiting for transfers between devices  13.3 us (11%)
  other arithmetic  5.48 us (5%)
  local copies, waits for them, and re-layouts  4.16 us (4%)
  between operations  1.64 us (1%)
    unnamed x1, blocking collectives  58.2 us
    ppermute x4, starting transfers between devices, extended(): lax.ppermute(lax.slice_in_dim(block, block.shape[dim] - width, None, axis...  17.6 us
    all_to_all x1, starting transfers between devices, local(): lax.all_to_all(current.astype(jnp.bfloat16), 'dates', split_axis=2, conca...  8.89 us
    ppermute x4, waiting for transfers between devices, extended(): lax.ppermute(lax.slice_in_dim(block, 0, width, axis=dim), axis, backward)  7.26 us
    all_to_all x1, waiting for transfers between devices, local(): lax.all_to_all(current.astype(jnp.bfloat16), 'dates', split_axis=2, conca...  6.04 us
    ppermute x4, starting transfers between devices, extended(): lax.ppermute(lax.slice_in_dim(block, 0, width, axis=dim), axis, backward)  5.17 us
    unnamed x10, local copies, waits for them, and re-layouts  3.14 us
  transfers between devices with their start and end apart: 9, of which 5 were waited for; matrix products, arithmetic and copies ran while one was open for 2% of the time, Pallas kernels for 0%

commit v1 on v0

v1 whole, which is shorter than its diff:
```python
import functools

import jax
import jax.numpy as jnp
from jax import lax
from jax.experimental import pallas as pl
from jax.experimental.pallas import tpu as pltpu
from jax.sharding import PartitionSpec as P

REGIONS = 8
STEPS = 4
LANES = 128

lam_space = 0.2
lam_time = 0.08


def edge_flux(difference):
    return difference * pl.reciprocal(1.0 + difference * difference)


def total(values):
    folded = jnp.sum(values.reshape(-1, 8, values.shape[-1]), axis=0)
    return jnp.sum(jnp.sum(folded, axis=0, keepdims=True), axis=1, keepdims=True)


def kernel(
    n,
    scenes_ref, mask_ref, region_ref,
    flat_ref, similarity_ref,
    planes, outgoing, arrived, land, row_weight, col_weight,
    field_a, field_b, final, share, shares,
    send_sem, recv_sem, share_send_sem, share_recv_sem, own_sem,
):
    me = lax.axis_index("dates")
    date_dev, bands, rows, cols = scenes_ref.shape
    rows_dev = rows // n
    window = rows_dev + 2 * STEPS
    group = date_dev * bands
    dates_all = date_dev * n
    pair = 16 // group

    barrier = pltpu.get_barrier_semaphore()

    @pl.loop(1, n)
    def _(k):
        pl.semaphore_signal(barrier, inc=1, device_id={"dates": lax.rem(me + k, n)})

    region = region_ref[...]
    for t in range(date_dev):
        clear = mask_ref[t] > 0
        label = jnp.where(clear, region, -1)
        values = [scenes_ref[t, b].astype(jnp.float32) for b in range(bands)]
        means = [jnp.zeros((rows, cols), jnp.float32) for _ in range(bands)]
        for g in range(REGIONS):
            member = label == g
            scale = 1.0 / (total(jnp.where(member, 1.0, 0.0)) + 1.0)
            for b in range(bands):
                mean = total(jnp.where(member, values[b], 0.0)) * scale
                means[b] = jnp.where(member, mean, means[b])
        for b in range(bands):
            anomaly = jnp.where(clear, values[b] - means[b], 0.0)
            planes[pl.ds(t * bands + b, rows, stride=group), :] = anomaly
    margin = STEPS // pair
    outgoing[:margin] = jnp.zeros((margin, 16, cols), jnp.bfloat16)
    outgoing[margin + rows // pair:] = jnp.zeros((margin, 16, cols), jnp.bfloat16)
    outgoing[margin:margin + rows // pair] = (
        planes[...].reshape(rows // pair, 16, cols).astype(jnp.bfloat16)
    )

    pl.semaphore_wait(barrier, n - 1)

    def block_copy(target):
        return pltpu.make_async_remote_copy(
            src_ref=outgoing.at[pl.ds(target * (rows_dev // pair), window // pair)],
            dst_ref=arrived.at[me],
            send_sem=send_sem.at[target],
            recv_sem=recv_sem.at[me],
            device_id={"dates": target},
        )

    @pl.loop(1, n)
    def _(k):
        block_copy(lax.rem(me + k, n)).start()

    own = pltpu.make_async_copy(
        outgoing.at[pl.ds(me * (rows_dev // pair), window // pair)], arrived.at[me], own_sem
    )
    own.start()

    land[:STEPS, :] = jnp.zeros((STEPS, cols), jnp.float32)
    land[STEPS + rows:, :] = jnp.zeros((STEPS, cols), jnp.float32)
    land[STEPS:STEPS + rows, :] = jnp.where(region > 0, 1.0, 0.0)
    lane = lax.broadcasted_iota(jnp.int32, (8, cols), 1)
    here = [
        jnp.broadcast_to(land[pl.ds(me * rows_dev + r, 1), :], (8, cols)) for r in range(window)
    ]
    for r in range(window):
        after = pltpu.roll(here[r], cols - 1, 1)
        col_weight[r] = jnp.where(lane < cols - 1, lam_space * here[r] * after, 0.0)
        if r + 1 < window:
            row_weight[r] = lam_space * here[r] * here[r + 1]
    share[...] = jnp.zeros(share.shape, jnp.float32)
    field_a[n] = jnp.zeros(field_a.shape[1:], jnp.float32)
    field_b[n] = jnp.zeros(field_b.shape[1:], jnp.float32)

    own.wait()

    def arrival(source):
        return pltpu.make_async_remote_copy(
            src_ref=outgoing.at[pl.ds(0, window // pair)],
            dst_ref=arrived.at[source],
            send_sem=send_sem.at[source],
            recv_sem=recv_sem.at[source],
            device_id={"dates": source},
        )

    @pl.loop(1, n)
    def _(k):
        arrival(lax.rem(me + k, n)).wait_recv()

    @pl.loop(0, n)
    def _(i):
        field_a[i] = arrived[i].astype(jnp.float32).reshape(window, 8, cols)

    upper = lax.broadcasted_iota(jnp.int32, (8, cols), 0) >= bands
    source, target = field_a, field_b
    for step in range(1, STEPS + 1):
        low, high = step, window - step
        count = high - low

        def body(i, before, source=source, target=target, low=low, high=high, step=step, count=count):
            wide = source[i, low - 1:high + 1]
            current = wide[1:-1]
            later = source[i + 1, low:high]
            row_flux = row_weight[low - 1:high] * edge_flux(wide[1:] - wide[:-1])
            right = pltpu.roll(current.reshape(count * 8, cols), cols - 1, 1).reshape(count, 8, cols)
            col_flux = col_weight[low:high] * edge_flux(right - current)
            col_before = pltpu.roll(col_flux.reshape(count * 8, cols), 1, 1).reshape(count, 8, cols)
            following = pltpu.roll(jnp.where(upper, current, later), 4, 1)
            last = jnp.where(i < n - 1, lam_time, 0.0)
            date_flux = jnp.where(upper, last, lam_time) * edge_flux(following - current)
            date_before = pltpu.roll(jnp.where(upper, before, date_flux), 4, 1)
            result = (
                current
                + (row_flux[1:] - row_flux[:-1])
                + (col_flux - col_before)
                + (date_flux - date_before)
            )
            if step < STEPS:
                target[i, low:high] = result
            else:
                for r in range(rows_dev):
                    start = pl.multiple_of((r * n + i) * 8, 8)
                    final[pl.ds(start, 8), :] = result[r]
            return date_flux

        lax.fori_loop(0, n, body, jnp.zeros((count, 8, cols), jnp.float32))
        source, target = target, source

    for b in range(bands):
        for r in range(rows_dev):
            column = (b * rows_dev + r) * cols
            flat_ref[:, column:column + cols] = final[
                pl.ds(r * n * 8 + b, dates_all, stride=bands), :
            ].astype(jnp.bfloat16)
    flat = flat_ref[...]
    product = lax.dot_general(
        flat, flat, (((1,), (1,)), ((), ())), preferred_element_type=jnp.float32
    )
    for j in range(n):
        share[j, :date_dev, :dates_all] = product[j * date_dev:(j + 1) * date_dev]

    def share_copy(target):
        return pltpu.make_async_remote_copy(
            src_ref=share.at[target],
            dst_ref=shares.at[me],
            send_sem=share_send_sem.at[target],
            recv_sem=share_recv_sem.at[me],
            device_id={"dates": target},
        )

    @pl.loop(1, n)
    def _(k):
        share_copy(lax.rem(me + k, n)).start()

    shares[me] = share[me]

    def share_arrival(source):
        return pltpu.make_async_remote_copy(
            src_ref=share.at[source],
            dst_ref=shares.at[source],
            send_sem=share_send_sem.at[source],
            recv_sem=share_recv_sem.at[source],
            device_id={"dates": source},
        )

    @pl.loop(1, n)
    def _(k):
        share_arrival(lax.rem(me + k, n)).wait_recv()

    summed = jnp.sum(shares[...], axis=0) * (1.0 / (bands * rows * cols))
    similarity_ref[...] = summed[:date_dev, :dates_all]

    @pl.loop(1, n)
    def _(k):
        block_copy(lax.rem(me + k, n)).wait_send()
        share_copy(lax.rem(me + k, n)).wait_send()


def local(n, scenes, cloud_mask, region):
    date_dev, bands, rows, cols = scenes.shape
    rows_dev = rows // n
    window = rows_dev + 2 * STEPS
    group = date_dev * bands
    pair = 16 // group
    dates_all = date_dev * n
    wide = max(LANES, dates_all)
    vmem = pl.BlockSpec(memory_space=pltpu.VMEM)
    flat, similarity = pl.pallas_call(
        functools.partial(kernel, n),
        out_shape=(
            jax.ShapeDtypeStruct((dates_all, bands * rows_dev * cols), jnp.bfloat16),
            jax.ShapeDtypeStruct((date_dev, dates_all), jnp.float32),
        ),
        in_specs=[vmem] * 3,
        out_specs=(vmem, vmem),
        scratch_shapes=[
            pltpu.VMEM((rows * group, cols), jnp.float32),
            pltpu.VMEM(((rows + 2 * STEPS) // pair, 16, cols), jnp.bfloat16),
            pltpu.VMEM((n, window // pair, 16, cols), jnp.bfloat16),
            pltpu.VMEM((rows + 2 * STEPS, cols), jnp.float32),
            pltpu.VMEM((window, 8, cols), jnp.float32),
            pltpu.VMEM((window, 8, cols), jnp.float32),
            pltpu.VMEM((n + 1, window, 8, cols), jnp.float32),
            pltpu.VMEM((n + 1, window, 8, cols), jnp.float32),
            pltpu.VMEM((rows_dev * n * 8, cols), jnp.float32),
            pltpu.VMEM((n, 8, wide), jnp.float32),
            pltpu.VMEM((n, 8, wide), jnp.float32),
            pltpu.SemaphoreType.DMA((n,)),
            pltpu.SemaphoreType.DMA((n,)),
            pltpu.SemaphoreType.DMA((n,)),
            pltpu.SemaphoreType.DMA((n,)),
            pltpu.SemaphoreType.DMA,
        ],
        compiler_params=pltpu.CompilerParams(
            collective_id=0, has_side_effects=True, vmem_limit_bytes=44 * 2**20
        ),
    )(scenes, cloud_mask, region)
    return flat.reshape(dates_all, bands, rows_dev, cols), similarity


def solution(mesh):
    in_specs = (
        P(("groups", "dates"), None, None, None),
        P(("groups", "dates"), None, None),
        P("groups", None),
    )
    out_specs = (P("groups", None, "dates", None), P(("groups", "dates"), None))
    return jax.shard_map(
        functools.partial(local, mesh.shape["dates"]),
        mesh=mesh, in_specs=in_specs, out_specs=out_specs, check_vma=False,
    )
```

time: 116 us -> 36.5 us (0.31)
  blocking collectives: 58.2 us -> 0 us
  Pallas kernels: 0 us -> 31.8 us
  starting transfers between devices: 31.7 us -> 0 us
  waiting for transfers between devices: 13.3 us -> 0 us
  other arithmetic: 5.48 us -> 0 us
    unnamed x1 -> x0, blocking collectives: 58.2 us -> none
    pallas_call x0 -> x1, Pallas kernels: none -> 31.8 us  [local(): pl.pallas_call(functools.partial(kernel, n), out_shape=(jax.ShapeDtypeStr...]
    ppermute x8 -> x0, starting transfers between devices: 22.8 us -> none  [the longest x4 17.6 us: extended(): lax.ppermute(lax.slice_in_dim(block, block.shape[dim] - width, None, axis...]
    all_to_all x1 -> x0, starting transfers between devices: 8.89 us -> none  [local(): lax.all_to_all(current.astype(jnp.bfloat16), 'dates', split_axis=2, conca...]
    ppermute x8 -> x0, waiting for transfers between devices: 7.27 us -> none  [the longest x4 7.26 us: extended(): lax.ppermute(lax.slice_in_dim(block, 0, width, axis=dim), axis, backward)]
    all_to_all x1 -> x0, waiting for transfers between devices: 6.04 us -> none  [local(): lax.all_to_all(current.astype(jnp.bfloat16), 'dates', split_axis=2, conca...]
    mul x16 -> x0, other arithmetic: 2.74 us -> none  [the longest x5 1.49 us: advance(): lam_space * col_weight]
    convert_element_type x9 -> x0, other arithmetic: 2.65 us -> none  [the longest x4 1.04 us: local(): current.astype(jnp.bfloat16)]
  transfers between devices with their start and end apart: 9 -> 0, of which waited for: 5 -> 0; matrix products, arithmetic and copies ran while one was open for 2% -> 0% of each run, Pallas kernels for 0% -> 0%
where the time goes in v1:
time: 36.5 us; the launch traced here: 36.2 us
  Pallas kernels  31.8 us (87%)
  local copies, waits for them, and re-layouts  3.78 us (10%)
  between operations  0.65 us (2%)
    pallas_call x1, Pallas kernels, local(): pl.pallas_call(functools.partial(kernel, n), out_shape=(jax.ShapeDtypeStr...  31.8 us
    unnamed x7, local copies, waits for them, and re-layouts  3.06 us

profile of v1, /device:TPU:0, one launch (start us, length us, event | category | flops | bytes accessed | tf_op | source)
XLA Modules:
  0.0 36.2 jit_solution(14219852752462770820)
XLA Ops:
  0.6 0.0 copy-start
  0.6 0.9 %copy-done = bf16[2,4,64,128]{3,2,1,0:T(8,128)(2,1)S(1)} copy-done((bf16[2,4,64,128]{3,2,1,0:T(8,128)(2,1)S(1)}, bf16[2,4,64,128]{3,2,1,0:T(8,128)(2,1)}, u32[]{:S(2)}) %copy-start) | copy-done | bytes 131096
  1.5 0.0 copy-start.1
  1.5 0.8 %copy-done.1 = s32[2,64,128]{2,1,0:T(8,128)S(1)} copy-done((s32[2,64,128]{2,1,0:T(8,128)S(1)}, s32[2,64,128]{2,1,0:T(8,128)}, u32[]{:S(2)}) %copy-start.1) | copy-done | bytes 65560
  2.4 0.0 copy-start.2
  2.4 0.8 %copy-done.2 = s32[64,128]{1,0:T(8,128)S(1)} copy-done((s32[64,128]{1,0:T(8,128)S(1)}, s32[64,128]{1,0:T(8,128)}, u32[]{:S(2)}) %copy-start.2) | copy-done | bytes 32792
  3.1 31.8 %shard_map.50 = (bf16[32,2048]{1,0:T(8,128)(2,1)S(1)}, f32[2,32]{1,0:T(2,128)S(1)}) custom-call(bf16[2,4,64,128]{3,2,1,0:T(8,128)(2,1)S(1)} %copy-done, s32[2,64,128]{2,1,0:T(8,128)S(1)} %copy-done.1, s32[64,128]{1,0:T(8,128)S(1)} %copy-done.2), custom_call_target="tpu_custom_call" | custom-call | tf_op jit(solution)/shard_map/pallas_call | solution.py:220
  34.9 0.7 %reshape.7 = bf16[32,4,4,128]{3,2,1,0:T(4,128)(2,1)} reshape(bf16[32,2048]{1,0:T(8,128)(2,1)S(1)} %get-tuple-element.4) | data formatting | bytes 262144 | tf_op jit(solution)/shard_map/reshape | solution.py:250
  35.6 0.6 %copy.6 = f32[2,32]{1,0:T(2,128)} copy(f32[2,32]{1,0:T(2,128)S(1)} %get-tuple-element.9) | data formatting | bytes 512
Async XLA Ops:
  0.6 0.9 %copy-start = (bf16[2,4,64,128]{3,2,1,0:T(8,128)(2,1)S(1)}, bf16[2,4,64,128]{3,2,1,0:T(8,128)(2,1)}, u32[]{:S(2)}) copy-start(bf16[2,4,64,128]{3,2,1,0:T(8,128)(2,1)} %scenes_ref.1) | copy-start | bytes 393220
  1.5 0.8 %copy-start.1 = (s32[2,64,128]{2,1,0:T(8,128)S(1)}, s32[2,64,128]{2,1,0:T(8,128)}, u32[]{:S(2)}) copy-start(s32[2,64,128]{2,1,0:T(8,128)} %mask_ref.1) | copy-start | bytes 196612
  2.4 0.8 %copy-start.2 = (s32[64,128]{1,0:T(8,128)S(1)}, s32[64,128]{1,0:T(8,128)}, u32[]{:S(2)}) copy-start(s32[64,128]{1,0:T(8,128)} %region_ref.1) | copy-start | bytes 98308

commit v2 on v1

--- a/solution.py
+++ b/solution.py
@@ -16,7 +16,7 @@
 
 
 def edge_flux(difference):
-    return difference * pl.reciprocal(1.0 + difference * difference)
+    return difference * pl.reciprocal(1.0 + difference * difference, approx=True)
 
 
 def total(values):
@@ -26,11 +26,11 @@
 
 def kernel(
     n,
-    scenes_ref, mask_ref, region_ref,
+    scenes_hbm, mask_hbm, region_hbm,
     flat_ref, similarity_ref,
-    planes, outgoing, arrived, land, row_weight, col_weight,
+    scenes_ref, mask_ref, region_ref, planes, outgoing, arrived, land, row_weight, col_weight,
     field_a, field_b, final, share, shares,
-    send_sem, recv_sem, share_send_sem, share_recv_sem, own_sem,
+    send_sem, recv_sem, share_send_sem, share_recv_sem, own_sem, load_sem,
 ):
     me = lax.axis_index("dates")
     date_dev, bands, rows, cols = scenes_ref.shape
@@ -40,12 +40,22 @@
     dates_all = date_dev * n
     pair = 16 // group
 
+    loads = [
+        pltpu.make_async_copy(source, target, load_sem.at[i])
+        for i, (source, target) in enumerate(
+            ((scenes_hbm, scenes_ref), (mask_hbm, mask_ref), (region_hbm, region_ref))
+        )
+    ]
+    for load in loads:
+        load.start()
     barrier = pltpu.get_barrier_semaphore()
 
     @pl.loop(1, n)
     def _(k):
         pl.semaphore_signal(barrier, inc=1, device_id={"dates": lax.rem(me + k, n)})
 
+    for load in loads:
+        load.wait()
     region = region_ref[...]
     for t in range(date_dev):
         clear = mask_ref[t] > 0
@@ -81,7 +91,8 @@
 
     @pl.loop(1, n)
     def _(k):
-        block_copy(lax.rem(me + k, n)).start()
+        ahead = n // 2 + (k // 2) * (1 - 2 * (k % 2))
+        block_copy(lax.rem(me + ahead, n)).start()
 
     own = pltpu.make_async_copy(
         outgoing.at[pl.ds(me * (rows_dev // pair), window // pair)], arrived.at[me], own_sem
@@ -105,6 +116,7 @@
     field_b[n] = jnp.zeros(field_b.shape[1:], jnp.float32)
 
     own.wait()
+    field_a[me] = arrived[me].astype(jnp.float32).reshape(window, 8, cols)
 
     def arrival(source):
         return pltpu.make_async_remote_copy(
@@ -117,10 +129,8 @@
 
     @pl.loop(1, n)
     def _(k):
-        arrival(lax.rem(me + k, n)).wait_recv()
-
-    @pl.loop(0, n)
-    def _(i):
+        i = lax.rem(me + k, n)
+        arrival(i).wait_recv()
         field_a[i] = arrived[i].astype(jnp.float32).reshape(window, 8, cols)
 
     upper = lax.broadcasted_iota(jnp.int32, (8, cols), 0) >= bands
@@ -223,9 +233,12 @@
             jax.ShapeDtypeStruct((dates_all, bands * rows_dev * cols), jnp.bfloat16),
             jax.ShapeDtypeStruct((date_dev, dates_all), jnp.float32),
         ),
-        in_specs=[vmem] * 3,
+        in_specs=[pl.BlockSpec(memory_space=pltpu.HBM)] * 3,
         out_specs=(vmem, vmem),
         scratch_shapes=[
+            pltpu.VMEM(scenes.shape, scenes.dtype),
+            pltpu.VMEM(cloud_mask.shape, cloud_mask.dtype),
+            pltpu.VMEM(region.shape, region.dtype),
             pltpu.VMEM((rows * group, cols), jnp.float32),
             pltpu.VMEM(((rows + 2 * STEPS) // pair, 16, cols), jnp.bfloat16),
             pltpu.VMEM((n, window // pair, 16, cols), jnp.bfloat16),
@@ -242,11 +255,12 @@
             pltpu.SemaphoreType.DMA((n,)),
             pltpu.SemaphoreType.DMA((n,)),
             pltpu.SemaphoreType.DMA,
+            pltpu.SemaphoreType.DMA((3,)),
         ],
         compiler_params=pltpu.CompilerParams(
             collective_id=0, has_side_effects=True, vmem_limit_bytes=44 * 2**20
         ),
-    )(scenes, cloud_mask, region)
+    )(*(pltpu.with_memory_space_constraint(x, pltpu.HBM) for x in (scenes, cloud_mask, region)))
     return flat.reshape(dates_all, bands, rows_dev, cols), similarity
 
 

time: 36.5 us -> 32.8 us (0.90)
  local copies, waits for them, and re-layouts: 3.78 us -> 1.29 us
  Pallas kernels: 31.8 us -> 30.8 us
    unnamed x7 -> x1, local copies, waits for them, and re-layouts: 3.06 us -> 0.56 us
    pallas_call x1, Pallas kernels: 31.8 us -> 30.8 us  [local(): pl.pallas_call(functools.partial(kernel, n), out_shape=(jax.ShapeDtypeStr...]
where the time goes in v2:
time: 32.8 us; the launch traced here: 32.7 us
  Pallas kernels  30.8 us (94%)
  local copies, waits for them, and re-layouts  1.29 us (4%)
  between operations  0.64 us (2%)
    pallas_call x1, Pallas kernels, local(): pl.pallas_call(functools.partial(kernel, n), out_shape=(jax.ShapeDtypeStr...  30.8 us
    reshape x1, local copies, waits for them, and re-layouts, local(): return (flat.reshape(dates_all, bands, rows_dev, cols), similarity)  0.73 us

profile of v2, /device:TPU:0, one launch (start us, length us, event | category | flops | bytes accessed | tf_op | source)
XLA Modules:
  0.0 32.7 jit_solution(4986610874500903895)
XLA Ops:
  0.6 30.8 %shard_map.50 = (bf16[32,2048]{1,0:T(8,128)(2,1)S(1)}, f32[2,32]{1,0:T(2,128)S(1)}) custom-call(bf16[2,4,64,128]{3,2,1,0:T(8,128)(2,1)} %scenes_hbm.1, s32[2,64,128]{2,1,0:T(8,128)} %mask_hbm.1, s32[64,128]{1,0:T(8,128)} %region_hbm.1), custom_call_target="tpu_custom_call" | custom-call | tf_op jit(solution)/shard_map/pallas_call | solution.py:230
  31.4 0.7 %reshape.7 = bf16[32,4,4,128]{3,2,1,0:T(4,128)(2,1)} reshape(bf16[32,2048]{1,0:T(8,128)(2,1)S(1)} %get-tuple-element.4) | data formatting | bytes 262144 | tf_op jit(solution)/shard_map/reshape | solution.py:264
  32.1 0.6 %copy.6 = f32[2,32]{1,0:T(2,128)} copy(f32[2,32]{1,0:T(2,128)S(1)} %get-tuple-element.9) | data formatting | bytes 512

commit v3 on v2

--- a/solution.py
+++ b/solution.py
@@ -31,6 +31,7 @@
     scenes_ref, mask_ref, region_ref, planes, outgoing, arrived, land, row_weight, col_weight,
     field_a, field_b, final, share, shares,
     send_sem, recv_sem, share_send_sem, share_recv_sem, own_sem, load_sem,
+    pass_send_sem, pass_recv_sem,
 ):
     me = lax.axis_index("dates")
     date_dev, bands, rows, cols = scenes_ref.shape
@@ -80,19 +81,38 @@
 
     pl.semaphore_wait(barrier, n - 1)
 
-    def block_copy(target):
-        return pltpu.make_async_remote_copy(
-            src_ref=outgoing.at[pl.ds(target * (rows_dev // pair), window // pair)],
-            dst_ref=arrived.at[me],
+    halo, depth = STEPS // pair, rows_dev // pair
+    chips, chip, odd = n // 2, me // 2, lax.rem(me, 2)
+    partner = me + 1 - 2 * odd
+
+    def ahead(k):
+        return chips // 2 + (k // 2) * (1 - 2 * lax.rem(k, 2))
+
+    def block_copy(target, core):
+        return pltpu.make_async_remote_copy(
+            src_ref=outgoing.at[pl.ds(target * depth + core * halo, depth + halo)],
+            dst_ref=arrived.at[me, pl.ds(core * halo, depth + halo)],
             send_sem=send_sem.at[target],
             recv_sem=recv_sem.at[me],
             device_id={"dates": target},
         )
 
-    @pl.loop(1, n)
-    def _(k):
-        ahead = n // 2 + (k // 2) * (1 - 2 * (k % 2))
-        block_copy(lax.rem(me + ahead, n)).start()
+    def partner_copy():
+        return pltpu.make_async_remote_copy(
+            src_ref=outgoing.at[pl.ds(partner * depth, window // pair)],
+            dst_ref=arrived.at[me],
+            send_sem=send_sem.at[partner],
+            recv_sem=recv_sem.at[me],
+            device_id={"dates": partner},
+        )
+
+    @pl.loop(1, chips)
+    def _(k):
+        other = lax.rem(chip + ahead(k), chips)
+        for core in range(2):
+            block_copy(2 * other + core, core).start()
+
+    partner_copy().start()
 
     own = pltpu.make_async_copy(
         outgoing.at[pl.ds(me * (rows_dev // pair), window // pair)], arrived.at[me], own_sem
@@ -120,18 +140,54 @@
 
     def arrival(source):
         return pltpu.make_async_remote_copy(
-            src_ref=outgoing.at[pl.ds(0, window // pair)],
-            dst_ref=arrived.at[source],
+            src_ref=outgoing.at[pl.ds(0, depth + halo)],
+            dst_ref=arrived.at[source, pl.ds(odd * halo, depth + halo)],
             send_sem=send_sem.at[source],
             recv_sem=recv_sem.at[source],
             device_id={"dates": source},
         )
 
-    @pl.loop(1, n)
-    def _(k):
-        i = lax.rem(me + k, n)
-        arrival(i).wait_recv()
-        field_a[i] = arrived[i].astype(jnp.float32).reshape(window, 8, cols)
+    def pass_on(source):
+        return pltpu.make_async_remote_copy(
+            src_ref=arrived.at[source, pl.ds(depth + odd * (halo - depth), halo)],
+            dst_ref=arrived.at[source, pl.ds(odd * (depth + halo), halo)],
+            send_sem=pass_send_sem.at[source],
+            recv_sem=pass_recv_sem.at[source],
+            device_id={"dates": partner},
+        )
+
+    def passed(source):
+        return pltpu.make_async_remote_copy(
+            src_ref=outgoing.at[pl.ds(0, halo)],
+            dst_ref=arrived.at[source, pl.ds((1 - odd) * (depth + halo), halo)],
+            send_sem=pass_send_sem.at[source],
+            recv_sem=pass_recv_sem.at[source],
+            device_id={"dates": partner},
+        )
+
+    @pl.loop(1, chips)
+    def _(k):
+        other = lax.rem(chip + chips - ahead(k), chips)
+        for core in range(2):
+            arrival(2 * other + core).wait_recv()
+            pass_on(2 * other + core).start()
+
+    pltpu.make_async_remote_copy(
+        src_ref=outgoing.at[pl.ds(0, window // pair)],
+        dst_ref=arrived.at[partner],
+        send_sem=send_sem.at[partner],
+        recv_sem=recv_sem.at[partner],
+        device_id={"dates": partner},
+    ).wait_recv()
+    field_a[partner] = arrived[partner].astype(jnp.float32).reshape(window, 8, cols)
+
+    @pl.loop(1, chips)
+    def _(k):
+        other = lax.rem(chip + chips - ahead(k), chips)
+        for core in range(2):
+            i = 2 * other + core
+            passed(i).wait_recv()
+            field_a[i] = arrived[i].astype(jnp.float32).reshape(window, 8, cols)
 
     upper = lax.broadcasted_iota(jnp.int32, (8, cols), 0) >= bands
     source, target = field_a, field_b
@@ -214,8 +270,16 @@
 
     @pl.loop(1, n)
     def _(k):
-        block_copy(lax.rem(me + k, n)).wait_send()
         share_copy(lax.rem(me + k, n)).wait_send()
+
+    @pl.loop(1, chips)
+    def _(k):
+        other = lax.rem(chip + k, chips)
+        for core in range(2):
+            block_copy(2 * other + core, core).wait_send()
+            pass_on(2 * other + core).wait_send()
+
+    partner_copy().wait_send()
 
 
 def local(n, scenes, cloud_mask, region):
@@ -256,6 +320,8 @@
             pltpu.SemaphoreType.DMA((n,)),
             pltpu.SemaphoreType.DMA,
             pltpu.SemaphoreType.DMA((3,)),
+            pltpu.SemaphoreType.DMA((n,)),
+            pltpu.SemaphoreType.DMA((n,)),
         ],
         compiler_params=pltpu.CompilerParams(
             collective_id=0, has_side_effects=True, vmem_limit_bytes=44 * 2**20

time: 32.8 us -> 31.8 us (0.970)
  Pallas kernels: 30.8 us -> 29.8 us
    pallas_call x1, Pallas kernels: 30.8 us -> 29.8 us  [local(): pl.pallas_call(functools.partial(kernel, n), out_shape=(jax.ShapeDtypeStr...]
where the time goes in v3:
time: 31.8 us; the launch traced here: 31.7 us
  Pallas kernels  29.8 us (94%)
  local copies, waits for them, and re-layouts  1.29 us (4%)
  between operations  0.64 us (2%)
    pallas_call x1, Pallas kernels, local(): pl.pallas_call(functools.partial(kernel, n), out_shape=(jax.ShapeDtypeStr...  29.8 us
    reshape x1, local copies, waits for them, and re-layouts, local(): return (flat.reshape(dates_all, bands, rows_dev, cols), similarity)  0.73 us

profile of v3, /device:TPU:0, one launch (start us, length us, event | category | flops | bytes accessed | tf_op | source)
XLA Modules:
  0.0 31.7 jit_solution(825381212284102946)
XLA Ops:
  0.6 29.8 %shard_map.50 = (bf16[32,2048]{1,0:T(8,128)(2,1)S(1)}, f32[2,32]{1,0:T(2,128)S(1)}) custom-call(bf16[2,4,64,128]{3,2,1,0:T(8,128)(2,1)} %scenes_hbm.1, s32[2,64,128]{2,1,0:T(8,128)} %mask_hbm.1, s32[64,128]{1,0:T(8,128)} %region_hbm.1), custom_call_target="tpu_custom_call" | custom-call | tf_op jit(solution)/shard_map/pallas_call | solution.py:294
  30.4 0.7 %reshape.7 = bf16[32,4,4,128]{3,2,1,0:T(4,128)(2,1)} reshape(bf16[32,2048]{1,0:T(8,128)(2,1)S(1)} %get-tuple-element.4) | data formatting | bytes 262144 | tf_op jit(solution)/shard_map/reshape | solution.py:330
  31.1 0.6 %copy.6 = f32[2,32]{1,0:T(2,128)} copy(f32[2,32]{1,0:T(2,128)S(1)} %get-tuple-element.9) | data formatting | bytes 512

commit v4 on v3

--- a/solution.py
+++ b/solution.py
@@ -19,9 +19,9 @@
     return difference * pl.reciprocal(1.0 + difference * difference, approx=True)
 
 
-def total(values):
-    folded = jnp.sum(values.reshape(-1, 8, values.shape[-1]), axis=0)
-    return jnp.sum(jnp.sum(folded, axis=0, keepdims=True), axis=1, keepdims=True)
+def totals(planes):
+    folded = [jnp.sum(plane.reshape(-1, 8, plane.shape[-1]), axis=0) for plane in planes]
+    return jnp.sum(jnp.sum(jnp.stack(folded), axis=1), axis=1, keepdims=True)
 
 
 def kernel(
@@ -62,13 +62,15 @@
         clear = mask_ref[t] > 0
         label = jnp.where(clear, region, -1)
         values = [scenes_ref[t, b].astype(jnp.float32) for b in range(bands)]
-        means = [jnp.zeros((rows, cols), jnp.float32) for _ in range(bands)]
-        for g in range(REGIONS):
-            member = label == g
-            scale = 1.0 / (total(jnp.where(member, 1.0, 0.0)) + 1.0)
-            for b in range(bands):
-                mean = total(jnp.where(member, values[b], 0.0)) * scale
-                means[b] = jnp.where(member, mean, means[b])
+        counts = totals([jnp.where(label == g, 1.0, 0.0) for g in range(REGIONS)])
+        means = []
+        for b in range(bands):
+            sums = totals([jnp.where(label == g, values[b], 0.0) for g in range(REGIONS)])
+            table = jnp.broadcast_to(sums / (counts + 1.0), (REGIONS, cols))
+            mean = jnp.zeros((rows, cols), jnp.float32)
+            for g in range(REGIONS):
+                mean = jnp.where(label == g, table[g:g + 1], mean)
+            means.append(mean)
         for b in range(bands):
             anomaly = jnp.where(clear, values[b] - means[b], 0.0)
             planes[pl.ds(t * bands + b, rows, stride=group), :] = anomaly

time: 31.8 us -> 31.8 us (level)
  no operation moved by 1% of the time
where the time goes in v4:
time: 31.8 us; the launch traced here: 31.7 us
  Pallas kernels  29.8 us (94%)
  local copies, waits for them, and re-layouts  1.29 us (4%)
  between operations  0.64 us (2%)
    pallas_call x1, Pallas kernels, local(): pl.pallas_call(functools.partial(kernel, n), out_shape=(jax.ShapeDtypeStr...  29.8 us
    reshape x1, local copies, waits for them, and re-layouts, local(): return (flat.reshape(dates_all, bands, rows_dev, cols), similarity)  0.73 us

profile of v4, /device:TPU:0, one launch (start us, length us, event | category | flops | bytes accessed | tf_op | source)
XLA Modules:
  0.0 31.7 jit_solution(5079417623013043411)
XLA Ops:
  0.6 29.8 %shard_map.50 = (bf16[32,2048]{1,0:T(8,128)(2,1)S(1)}, f32[2,32]{1,0:T(2,128)S(1)}) custom-call(bf16[2,4,64,128]{3,2,1,0:T(8,128)(2,1)} %scenes_hbm.1, s32[2,64,128]{2,1,0:T(8,128)} %mask_hbm.1, s32[64,128]{1,0:T(8,128)} %region_hbm.1), custom_call_target="tpu_custom_call" | custom-call | tf_op jit(solution)/shard_map/pallas_call | solution.py:296
  30.4 0.7 %reshape.7 = bf16[32,4,4,128]{3,2,1,0:T(4,128)(2,1)} reshape(bf16[32,2048]{1,0:T(8,128)(2,1)S(1)} %get-tuple-element.4) | data formatting | bytes 262144 | tf_op jit(solution)/shard_map/reshape | solution.py:332
  31.1 0.6 %copy.6 = f32[2,32]{1,0:T(2,128)} copy(f32[2,32]{1,0:T(2,128)S(1)} %get-tuple-element.9) | data formatting | bytes 512

commit v5 on v3

--- a/solution.py
+++ b/solution.py
@@ -221,7 +221,7 @@
                     final[pl.ds(start, 8), :] = result[r]
             return date_flux
 
-        lax.fori_loop(0, n, body, jnp.zeros((count, 8, cols), jnp.float32))
+        lax.fori_loop(0, n, body, jnp.zeros((count, 8, cols), jnp.float32), unroll=2)
         source, target = target, source
 
     for b in range(bands):

time: 31.8 us -> 27 us (0.85)
  Pallas kernels: 29.8 us -> 24.9 us
    pallas_call x1, Pallas kernels: 29.8 us -> 24.9 us  [local(): pl.pallas_call(functools.partial(kernel, n), out_shape=(jax.ShapeDtypeStr...]
where the time goes in v5:
time: 27 us; the launch traced here: 26.9 us
  Pallas kernels  24.9 us (92%)
  local copies, waits for them, and re-layouts  1.29 us (5%)
  between operations  0.64 us (2%)
    pallas_call x1, Pallas kernels, local(): pl.pallas_call(functools.partial(kernel, n), out_shape=(jax.ShapeDtypeStr...  24.9 us
    reshape x1, local copies, waits for them, and re-layouts, local(): return (flat.reshape(dates_all, bands, rows_dev, cols), similarity)  0.73 us
    unnamed x1, local copies, waits for them, and re-layouts  0.56 us

profile of v5, /device:TPU:0, one launch (start us, length us, event | category | flops | bytes accessed | tf_op | source)
XLA Modules:
  0.0 26.9 jit_solution(8897351029525890628)
XLA Ops:
  0.6 24.9 %shard_map.50 = (bf16[32,2048]{1,0:T(8,128)(2,1)S(1)}, f32[2,32]{1,0:T(2,128)S(1)}) custom-call(bf16[2,4,64,128]{3,2,1,0:T(8,128)(2,1)} %scenes_hbm.1, s32[2,64,128]{2,1,0:T(8,128)} %mask_hbm.1, s32[64,128]{1,0:T(8,128)} %region_hbm.1), custom_call_target="tpu_custom_call" | custom-call | tf_op jit(solution)/shard_map/pallas_call | solution.py:294
  25.6 0.7 %reshape.7 = bf16[32,4,4,128]{3,2,1,0:T(4,128)(2,1)} reshape(bf16[32,2048]{1,0:T(8,128)(2,1)S(1)} %get-tuple-element.4) | data formatting | bytes 262144 | tf_op jit(solution)/shard_map/reshape | solution.py:330
  26.3 0.6 %copy.6 = f32[2,32]{1,0:T(2,128)} copy(f32[2,32]{1,0:T(2,128)S(1)} %get-tuple-element.9) | data formatting | bytes 512

commit v6 on v5

--- a/solution.py
+++ b/solution.py
@@ -221,7 +221,7 @@
                     final[pl.ds(start, 8), :] = result[r]
             return date_flux
 
-        lax.fori_loop(0, n, body, jnp.zeros((count, 8, cols), jnp.float32), unroll=2)
+        lax.fori_loop(0, n, body, jnp.zeros((count, 8, cols), jnp.float32), unroll=4)
         source, target = target, source
 
     for b in range(bands):

time: 27 us -> 24.9 us (0.922)
  Pallas kernels: 24.9 us -> 22.8 us
    pallas_call x1, Pallas kernels: 24.9 us -> 22.8 us  [local(): pl.pallas_call(functools.partial(kernel, n), out_shape=(jax.ShapeDtypeStr...]
where the time goes in v6:
time: 24.9 us; the launch traced here: 24.7 us
  Pallas kernels  22.8 us (92%)
  local copies, waits for them, and re-layouts  1.29 us (5%)
  between operations  0.64 us (3%)
    pallas_call x1, Pallas kernels, local(): pl.pallas_call(functools.partial(kernel, n), out_shape=(jax.ShapeDtypeStr...  22.8 us
    reshape x1, local copies, waits for them, and re-layouts, local(): return (flat.reshape(dates_all, bands, rows_dev, cols), similarity)  0.73 us
    unnamed x1, local copies, waits for them, and re-layouts  0.56 us

profile of v6, /device:TPU:0, one launch (start us, length us, event | category | flops | bytes accessed | tf_op | source)
XLA Modules:
  0.0 24.7 jit_solution(6778203714699583451)
XLA Ops:
  0.6 22.8 %shard_map.50 = (bf16[32,2048]{1,0:T(8,128)(2,1)S(1)}, f32[2,32]{1,0:T(2,128)S(1)}) custom-call(bf16[2,4,64,128]{3,2,1,0:T(8,128)(2,1)} %scenes_hbm.1, s32[2,64,128]{2,1,0:T(8,128)} %mask_hbm.1, s32[64,128]{1,0:T(8,128)} %region_hbm.1), custom_call_target="tpu_custom_call" | custom-call | tf_op jit(solution)/shard_map/pallas_call | solution.py:294
  23.4 0.7 %reshape.7 = bf16[32,4,4,128]{3,2,1,0:T(4,128)(2,1)} reshape(bf16[32,2048]{1,0:T(8,128)(2,1)S(1)} %get-tuple-element.4) | data formatting | bytes 262144 | tf_op jit(solution)/shard_map/reshape | solution.py:330
  24.2 0.6 %copy.6 = f32[2,32]{1,0:T(2,128)} copy(f32[2,32]{1,0:T(2,128)S(1)} %get-tuple-element.9) | data formatting | bytes 512
